TPU v7x, 256 devices: a whole 4x4x8 slice. The times are simulated.
256 devices in a mesh: grp: 4 (over x), blk: 64 (over z, y, core).
Axes of the slice: x: 4, y: 4, z: 8, core: 2. Of those that a mesh axis runs over, the one named last changes fastest.
Arguments:
- embeddings: bfloat16 [131072, 1024], P(('grp', 'blk')), may hold values from -6 to 6
- labels: int32 [131072], P(('grp', 'blk')), may hold values from 0 to 127, as said below
Outputs:
- best_match: float32 [131072], P(('grp', 'blk'))
Inputs may be any that keep to these rules, and one draw needn't show every extreme that they name: `labels`: in each aligned block of 512 rows (the rows of one device), the rows whose cluster has owner index b (label // 2 == b) number either 0 or exactly 16, for every b; one owner index per index of grp may receive 16 rows from every one of that grp index's 64 blocks, so a device can receive up to 1024 rows; other owners receive fewer.
All inputs are finite; a program needn't handle non-finite values.
Results may differ from a plain program's by a relative error of at most 0.0014.
Values may be sent and summed in bfloat16 or wider, within the bound.
A program may use at most 64 MiB of HBM per device.

v0:
```python
import jax
import jax.numpy as jnp
from jax import lax
from jax.sharding import PartitionSpec as P

CLUSTERS_PER_BLK = 2


def masked_tile(left, left_marks, right, right_marks, left_first):
    scores = jnp.dot(left, right.T, preferred_element_type=jnp.float32)
    here = left_first + jnp.arange(left.shape[0], dtype=jnp.int32)
    there = jnp.arange(right.shape[0], dtype=jnp.int32)
    keep = (
        (left_marks[:, None] == right_marks[None, :])
        & (left_marks[:, None] >= 0)
        & (here[:, None] != there[None, :])
    )
    return jnp.where(keep, scores, -1.0)


def shards(embeddings, labels):
    owners = lax.axis_size("blk")
    held = embeddings.shape[0]
    capacity = 2 * held // owners
    values = embeddings.astype(jnp.float32)
    unit = (values * lax.rsqrt(jnp.sum(values * values, axis=1, keepdims=True) + 1e-06)).astype(
        jnp.bfloat16
    )
    owner_index = labels // CLUSTERS_PER_BLK
    choose = (owner_index[:, None] == jnp.arange(owners, dtype=jnp.int32)[None, :]).astype(
        jnp.int32
    )
    position = jnp.sum(choose * (jnp.cumsum(choose, axis=0) - 1), axis=1)
    flat = owner_index * capacity + position
    outgoing = jnp.zeros((owners * capacity, unit.shape[1]), jnp.bfloat16).at[flat].set(unit)
    out_marks = jnp.full((owners * capacity,), -1, jnp.int32).at[flat].set(labels)
    incoming, in_marks = (
        lax.all_to_all(
            outgoing.reshape(owners, capacity, -1), "blk", split_axis=0, concat_axis=0, tiled=True
        ),
        lax.all_to_all(
            out_marks.reshape(owners, capacity), "blk", split_axis=0, concat_axis=0, tiled=True
        ),
    )
    mine = incoming.reshape(owners * capacity, -1)
    my_marks = in_marks.reshape(-1)
    count = mine.shape[0]
    my_first = lax.axis_index("grp") * count
    start_best = jnp.full((count,), -1.0, jnp.float32)
    tile = masked_tile(
        mine,
        my_marks,
        lax.all_gather(mine, "grp", axis=0, tiled=True),
        lax.all_gather(my_marks, "grp", axis=0, tiled=True),
        my_first,
    )
    best = jnp.maximum(start_best, jnp.max(tile, axis=1))
    back = lax.all_to_all(
        best.reshape(owners, capacity), "blk", split_axis=0, concat_axis=0, tiled=True
    )
    return back.reshape(-1)[flat]


def solution(mesh):
    in_specs = (P(("grp", "blk"), None), P(("grp", "blk")))
    out_specs = P(("grp", "blk"))
    return jax.shard_map(shards, mesh=mesh, in_specs=in_specs, out_specs=out_specs, check_vma=False)
```

profile of v0, /device:TPU:2, one launch (start us, length us, event | category | flops | bytes accessed | tf_op | source)
XLA Modules:
  0.0 209.1 jit_solution(534891691460932703)
XLA Ops:
  6.5 0.0 all-gather.2.cloned.1.call-start
  6.5 0.7 fusion.16
  7.2 0.7 add_select_fusion
  7.9 1.2 reduce-window.6
  9.1 0.2 slice_reduce_fusion
  9.4 0.1 fusion.8
  9.5 0.7 compare_select_fusion
  10.2 1.5 fusion.1
  11.7 4.0 %scatter_custom_fusion.1 = bf16[1024,1024]{1,0:T(8,128)(2,1)S(1)} fusion(s32[512]{0:T(512)S(1)} %compare_select_fusion, bf16[512,1024]{1,0:T(8,128)(2,1)} %param.2, f32[512]{0:T(512)S(1)} %add_rsqrt_fusion, bf16[]{:T(256)} %constant.41.clone.1), kind=kCustom, calls=%fused_computation.10 | custom fusion | flops 1572864 | bytes 3147778 | tf_op jit(solution)/shard_map/scatter | solution.py:35
  15.7 63.4 %all_to_all.20 = bf16[64,16,1024]{2,1,0:T(8,128)(2,1)} all-to-all(bf16[64,16,1024]{2,1,0:T(8,128)(2,1)S(1)} %bitcast.25), channel_id=1, replica_groups=mesh['grp'=4,'blk'=64] {'blk'}, dimensions={0} | all-to-all | bytes 4194304 | tf_op jit(solution)/shard_map/all_to_all | solution.py:38
  79.1 0.0 all-gather.2.cloned.1.call-update
  79.1 2.6 %scatter_custom_fusion = s32[1024]{0:T(1024)S(1)} fusion(s32[512]{0:T(512)S(1)} %compare_select_fusion, s32[512]{0:T(512)} %param.3, s32[]{:T(128)} %constant.14.clone.1), kind=kCustom, calls=%fused_computation.33 | custom fusion | bytes 4608 | tf_op jit(solution)/shard_map/scatter | solution.py:36
  81.7 0.7 all_to_all.13
  82.4 5.3 %all-to-all-start = ((s32[64,1,16]{2,1,0:T(1,128)}), s32[64,1,16]{2,1,0:T(1,128)S(1)}, u32[]{:S(2)}, u32[]{:S(2)}) async-start(s32[64,1,16]{2,1,0:T(1,128)} %bitcast.2), calls=%async_computation | async-start | bytes 65536 | tf_op jit(solution)/shard_map/all_to_all | solution.py:41
  87.8 9.6 %all-to-all-done = s32[64,1,16]{2,1,0:T(1,128)S(1)} async-done(((s32[64,1,16]{2,1,0:T(1,128)}), s32[64,1,16]{2,1,0:T(1,128)S(1)}, u32[]{:S(2)}, u32[]{:S(2)}) %all-to-all-start) | async-done | bytes 4128 | tf_op jit(solution)/shard_map/all_to_all | solution.py:41
  97.3 0.5 broadcast.84
  97.9 0.7 reduce.8
  98.6 0.1 eq.45
  98.7 12.2 %all_gather.6 = s32[4096]{0:T(1024)S(1)} all-gather(s32[1024]{0:T(1024)S(1)} %eq.45), channel_id=1, replica_groups=mesh['grp'=4,'blk'=64] {'grp'}, dimensions={0}, use_global_device_ids=true | all-gather | bytes 20480 | tf_op jit(solution)/shard_map/all_gather | solution.py:54
  110.8 50.4 %all-gather.2.cloned.1.call-done = bf16[4096,1024]{1,0:T(8,128)(2,1)} async-done(((bf16[1024,1024]{1,0:T(8,128)(2,1)}), bf16[4096,1024]{1,0:T(8,128)(2,1)}) %all-gather.2.cloned.1.call-update) | async-done | bytes 8388624 | tf_op jit(solution)/shard_map/all_gather | solution.py:53
  161.2 15.5 %select_reduce_fusion = f32[1024]{0:T(1024)S(1)} fusion(s32[1024]{0:T(1024)S(1)} %iota_add_fusion, s32[4096]{0:T(1024)S(1)} %all_gather.6, s32[1024]{0:T(1024)S(1)} %eq.45, pred[1024]{0:T(1024)(128)(4,1)S(1)} %broadcast_compare_fusion, bf16[1024,1024]{1,0:T(8,128)(2,1)} %bitcast.24, bf16[4096,1024]{1,0:T(8,128)(2,1)} %all-gather.2.cloned.1.call-done), kind=kOutput, calls=%fused_computation.3 | convolution fusion | flops 8615099392 | bytes 10515456 | tf_op jit(solution)/shard_map/dot_general | solution.py:10
  176.7 0.7 max_broadcast_in_dim.15
  177.4 10.5 %all-to-all-start.2 = ((f32[64,1,16]{2,1,0:T(1,128)}), f32[64,1,16]{2,1,0:T(1,128)S(1)}, u32[]{:S(2)}, u32[]{:S(2)}) async-start(f32[64,1,16]{2,1,0:T(1,128)} %bitcast.5), calls=%async_computation.2 | async-start | bytes 65536 | tf_op jit(solution)/shard_map/all_to_all | solution.py:58
  187.9 9.6 %all-to-all-done.2 = f32[64,1,16]{2,1,0:T(1,128)S(1)} async-done(((f32[64,1,16]{2,1,0:T(1,128)}), f32[64,1,16]{2,1,0:T(1,128)S(1)}, u32[]{:S(2)}, u32[]{:S(2)}) %all-to-all-start.2) | async-done | bytes 4128 | tf_op jit(solution)/shard_map/all_to_all | solution.py:58
  197.5 0.5 broadcast.85
  198.0 0.7 reduce.9
  198.7 0.1 reshape.74
  198.8 3.4 %gather_fusion = f32[512]{0:T(512)} fusion(f32[1024]{0:T(1024)S(1)} %reshape.74, s32[1024]{0:T(1024)S(1)} %pad_clamp_fusion), kind=kCustom, calls=%fused_computation | custom fusion | bytes 6144 | tf_op jit(solution)/shard_map/gather | solution.py:61
  (8 shorter events, 0.1 us)
Async XLA Ops:
  6.5 154.7 %all-gather.2.cloned.1.call-start = ((), (), s32[]{:S(2)}) async-start(), calls=%async_computation.3 | async-start | bytes 10485760 | tf_op jit(solution)/shard_map/all_gather | solution.py:53
  82.4 14.9 %all-to-all-start = ((s32[64,1,16]{2,1,0:T(1,128)}), s32[64,1,16]{2,1,0:T(1,128)S(1)}, u32[]{:S(2)}, u32[]{:S(2)}) async-start(s32[64,1,16]{2,1,0:T(1,128)} %bitcast.2), calls=%async_computation | async-start | bytes 65536 | tf_op jit(solution)/shard_map/all_to_all | solution.py:41
  177.4 20.1 %all-to-all-start.2 = ((f32[64,1,16]{2,1,0:T(1,128)}), f32[64,1,16]{2,1,0:T(1,128)S(1)}, u32[]{:S(2)}, u32[]{:S(2)}) async-start(f32[64,1,16]{2,1,0:T(1,128)} %bitcast.5), calls=%async_computation.2 | async-start | bytes 65536 | tf_op jit(solution)/shard_map/all_to_all | solution.py:58
Sparse Core Ops, SparseCore 0:
  79.2 81.9 all-gather.1
where the time goes:
time: 210 us; the launch traced here: 209 us
  blocking collectives  75.5 us (36%)
  waiting for transfers between devices  69.6 us (33%)
  starting transfers between devices  15.8 us (8%)
  matrix products  15.5 us (7%)
  between operations  13.5 us (6%)
  other arithmetic  10.4 us (5%)
  local copies, waits for them, and re-layouts  8.78 us (4%)
    all_to_all x1, blocking collectives, shards(): lax.all_to_all(outgoing.reshape(owners, capacity, -1), 'blk', split_axis=...  63.4 us
    all_gather x1, waiting for transfers between devices, shards(): lax.all_gather(mine, 'grp', axis=0, tiled=True)  50.4 us
    dot_general x1, matrix products, masked_tile(): scores = jnp.dot(left, right.T, preferred_element_type=jnp.float32)  15.5 us
    all_gather x1, blocking collectives, shards(): lax.all_gather(my_marks, 'grp', axis=0, tiled=True)  12.2 us
    all_to_all x1, starting transfers between devices, shards(): lax.all_to_all(best.reshape(owners, capacity), 'blk', split_axis=0, conca...  10.5 us
    all_to_all x1, waiting for transfers between devices, shards(): lax.all_to_all(out_marks.reshape(owners, capacity), 'blk', split_axis=0,...  9.59 us
    all_to_all x1, waiting for transfers between devices, shards(): lax.all_to_all(best.reshape(owners, capacity), 'blk', split_axis=0, conca...  9.57 us
    all_to_all x1, starting transfers between devices, shards(): lax.all_to_all(out_marks.reshape(owners, capacity), 'blk', split_axis=0,...  5.34 us
  transfers between devices with their start and end apart: 3, of which 3 were waited for; matrix products, arithmetic and copies ran while one was open for 2% of the time, Pallas kernels for 0%

commit v1 on v0

v1 whole, which is shorter than its diff:
```python
import functools

import jax
import jax.numpy as jnp
from jax import lax
from jax.experimental import pallas as pl
from jax.experimental.pallas import tpu as pltpu
from jax.sharding import PartitionSpec as P

MESH = pl.DeviceIdType.MESH
F32 = jnp.float32
BF16 = jnp.bfloat16

NX, NY, NZ = 4, 4, 8
CAP = 16
STEPS = 8
GROUP = 256
D = 1024


def place():
    x, b = lax.axis_index("grp"), lax.axis_index("blk")
    return x, lax.rem(lax.div(b, 2), NY), lax.div(b, 2 * NY), lax.rem(b, 2)


def device(x, y, z, c):
    return (x, z * (2 * NY) + y * 2 + c)


def z_offset(t):
    return jnp.where(lax.rem(t, 2) == 1, lax.div(t + 1, 2), lax.rem(NZ - lax.div(t, 2), NZ))


def remote(src, dst, send, recv, where):
    return pltpu.make_async_remote_copy(
        src_ref=src, dst_ref=dst, send_sem=send, recv_sem=recv, device_id=where, device_id_type=MESH
    )


def arrived(ref, sem):
    pltpu.make_async_copy(ref, ref, sem).wait()


def iota(shape, dim):
    return lax.broadcasted_iota(jnp.int32, shape, dim)


def kernel(
    emb_hbm, labels, out, emb, src, marks, rows, row_marks_in, row_marks, col_marks, best, result, results, back, backs,
    load_sem, send_sem, recv_sem, mark_send_sem, mark_recv_sem, pair_send_sem, pair_recv_sem, pair_mark_send_sem,
    pair_mark_recv_sem, result_send_sem, result_recv_sem, back_send_sem, back_recv_sem,
):
    x, y, z, c = place()
    parity = lax.rem(x + y + z, 2)
    is_owner = parity == 0
    pair = device(x, y, z, 1 - c)

    load = pltpu.make_async_copy(emb_hbm, emb, load_sem)
    load.start()
    barrier = pltpu.get_barrier_semaphore()

    @pl.when(is_owner)
    def _():
        def greet(n, carry):
            to = device(
                lax.rem(x + lax.rem(n, NX), NX), lax.rem(y + lax.rem(lax.div(n, NX), NY), NY),
                lax.rem(z + lax.div(n, NX * NY), NZ), c,
            )
            pl.semaphore_signal(barrier, inc=1, device_id=to, device_id_type=MESH)
            return carry

        lax.fori_loop(1, NX * NY * NZ, greet, 0)
        pl.semaphore_signal(barrier, inc=1, device_id=pair, device_id_type=MESH)

    held = emb.shape[0]
    owner_of = lax.div(labels[...], 2)
    chosen = (iota((64, held), 0) == owner_of).astype(F32)
    before = (iota((held, held), 0) < iota((held, held), 1)).astype(F32).astype(BF16)
    count = jnp.dot(chosen.astype(BF16), before, preferred_element_type=F32)
    position = jnp.sum(chosen * count, axis=0, keepdims=True).astype(jnp.int32)
    flat = owner_of * CAP + position
    at_lane = jnp.where(lax.rem(iota((128, held), 0), CAP) == position, 1 + lax.rem(labels[...], 2), 0).astype(F32)
    marks[...] = lax.dot_general(
        chosen.astype(BF16), at_lane.astype(BF16), (((1,), (1,)), ((), ())), preferred_element_type=F32
    )

    load.wait()

    def normalise(n, carry):
        part = pl.ds(n * 64, 64)
        values = emb[part, :].astype(F32)
        scale = lax.rsqrt(jnp.sum(values * values, axis=1, keepdims=True) + 1e-06)
        emb[part, :] = (values * scale).astype(BF16)
        return carry

    lax.fori_loop(0, held // 64, normalise, 0)

    def targets(i):
        out = []
        for j in range(8):
            dz = z_offset(lax.rem(i + j, 8))
            dy, h = j // 2, j % 2
            q = lax.rem(parity + dy + dz, 2)
            to = (lax.rem(x + 2 * h + q, NX), lax.rem(y + dy, NY), lax.rem(z + dz, NZ))
            out.append((to[2] * 8 + to[1] * 2 + lax.div(to[0], 2), q, device(*to, c)))
        return out

    def pack(i, to):
        chosen_rows = jnp.concatenate(
            [jnp.where(iota((CAP, held), 0) == flat - b * CAP, 1.0, 0.0) for b, _, _ in to], axis=0
        ).astype(BF16)
        src[pl.ds(pl.multiple_of(i * 128, 128), 128), :] = jnp.dot(
            chosen_rows, emb[...], preferred_element_type=F32
        ).astype(BF16)

    def copies(i, j, b, q):
        slot = 2 * j + q
        return (
            src.at[pl.ds(pl.multiple_of(i * 128 + j * CAP, CAP), CAP)],
            rows.at[i, pl.ds(pl.multiple_of(slot * CAP, CAP), CAP)],
            marks.at[pl.ds(b, 1)],
            row_marks_in.at[i, pl.ds(slot, 1)],
        )

    def send(i, j, b, q, where):
        s, d, ms, md = copies(i, j, b, q)
        remote(s, d, send_sem, recv_sem.at[i], where).start()
        remote(ms, md, mark_send_sem, mark_recv_sem.at[i], where).start()

    first = targets(0)
    pack(0, first)
    pl.semaphore_wait(barrier, 64)
    for j in range(8):
        b, q, where = first[j]
        if j == 0:

            @pl.when(is_owner)
            def _():
                s, d, ms, md = copies(0, 0, b, 0)
                pltpu.make_async_copy(s, d, recv_sem.at[0]).start()
                pltpu.make_async_copy(ms, md, mark_recv_sem.at[0]).start()

            @pl.when(jnp.logical_not(is_owner))
            def _():
                send(0, 0, b, q, where)
        else:
            send(0, j, b, q, where)

    def step(i, carry):
        to = targets(i)
        pack(i, to)
        for j in range(8):
            send(i, j, *to[j])
        return carry

    lax.fori_loop(1, STEPS, step, 0)

    @pl.when(is_owner)
    def _():
        best[...] = jnp.full(best.shape, -1.0, F32)
        lane = iota((16, 128), 1)
        mine = lax.div(lane, CAP) == lax.rem(iota((16, 128), 0), 8)
        diagonal = lax.rem(iota((16, CAP, 128), 2), 128) == iota((16, CAP, 128), 1)

        def spread(i, half):
            m = row_marks_in[i, pl.ds(half * 16, 16), :]
            column = jnp.sum(jnp.where(diagonal, m.reshape(16, 1, 128), 0.0), axis=2, keepdims=True)
            row_marks[i, pl.ds(half * GROUP, GROUP), :] = jnp.broadcast_to(column, (16, CAP, 128)).reshape(GROUP, 128)
            return m

        def tile(k, first_row, size, col, diag=False):
            left = rows[k, pl.ds(first_row, size), :]
            right = rows[col, pl.ds(0, GROUP), :]
            sim = lax.dot_general(left, right, (((1,), (1,)), ((), ())), preferred_element_type=F32)
            m = row_marks[k, pl.ds(first_row, size), :]
            keep = jnp.concatenate([m, m], axis=1) == col_marks[col, 0:1, :]
            if diag:
                keep = keep & (iota((size, GROUP), 0) != iota((size, GROUP), 1))
            sim = jnp.where(keep, sim, -1.0)
            best[col] = jnp.maximum(best[col], jnp.max(sim.reshape(size // 8, 8, GROUP), axis=0))

        def group(i, carry):
            arrived(rows.at[i, pl.ds(0, GROUP)], recv_sem.at[i])
            arrived(row_marks_in.at[i, pl.ds(0, 16)], mark_recv_sem.at[i])
            remote(
                rows.at[i, pl.ds(0, GROUP)], rows.at[i, pl.ds(GROUP, GROUP)], pair_send_sem, pair_recv_sem.at[i], pair
            ).start()
            remote(
                row_marks_in.at[i, pl.ds(0, 16)], row_marks_in.at[i, pl.ds(16, 16)], pair_mark_send_sem,
                pair_mark_recv_sem.at[i], pair,
            ).start()
            m = spread(i, 0)
            lanes = jnp.sum(jnp.where(mine, m, 0.0).reshape(2, 8, 128), axis=1)
            col_marks[i] = jnp.broadcast_to(jnp.concatenate([lanes[0:1], lanes[1:2]], axis=1), (8, GROUP))
            tile(i, 0, GROUP, i, diag=True)

            def earlier(k, carry):
                tile(k, 0, 2 * GROUP, i)
                tile(i, 0, GROUP, k)
                return carry

            lax.fori_loop(0, i, earlier, 0)
            arrived(rows.at[i, pl.ds(GROUP, GROUP)], pair_recv_sem.at[i])
            arrived(row_marks_in.at[i, pl.ds(16, 16)], pair_mark_recv_sem.at[i])
            spread(i, 1)

            def all_columns(k, carry):
                tile(i, GROUP, GROUP, k)
                return carry

            lax.fori_loop(0, i + 1, all_columns, 0)
            return carry

        lax.fori_loop(0, STEPS, group, 0)
        for i in range(STEPS):
            top = jnp.max(best[i], axis=0, keepdims=True)
            result[pl.ds(2 * i, 1), :] = top[:, 0:128]
            result[pl.ds(2 * i + 1, 1), :] = top[:, 128:256]
        me = y * 2 + lax.div(x, 2)
        pltpu.make_async_copy(result, results.at[me], result_recv_sem).start()
        for n in range(1, NX * NY):
            where = device(lax.rem(x + n % NX, NX), lax.rem(y + n // NX, NY), z, c)
            remote(result, results.at[me], result_send_sem, result_recv_sem, where).start()

    arrived(results, result_recv_sem)
    for o in range(8):
        oy = o // 2
        ox = 2 * (o % 2) + lax.rem(oy + z, 2)
        dx = lax.rem(ox - x + NX, NX)
        j = lax.rem(oy - y + NY, NY) * 2 + lax.div(dx, 2)

        def turn(t, carry):
            i = lax.rem(t - j + 8, 8)
            back[t, pl.ds(o, 1), :] = results[o, pl.ds(2 * i + lax.div(j, 4), 1), :]
            return carry

        lax.fori_loop(0, NZ, turn, 0)
    pltpu.make_async_copy(back.at[0], backs.at[z], back_recv_sem).start()
    for t in range(1, NZ):
        dz = (t + 1) // 2 if t % 2 else (NZ - t // 2) % NZ
        where = device(x, y, lax.rem(z - dz + NZ, NZ), c)
        remote(back.at[t], backs.at[z], back_send_sem, back_recv_sem, where).start()
    arrived(backs, back_recv_sem)

    b = iota((64, 128), 0)
    oz, oy = lax.div(b, 8), lax.rem(lax.div(b, 2), NY)
    ox = 2 * lax.rem(b, 2) + lax.rem(oy + oz, 2)
    dx = lax.rem(ox - x + NX, NX)
    j = lax.rem(oy - y + NY, NY) * 2 + lax.div(dx, 2)
    ours = lax.div(iota((64, 128), 1), CAP) == lax.rem(j, 4) * 2 + lax.rem(dx, 2)
    left = jnp.where(ours, backs[...].reshape(64, 128), 0.0)
    left = jnp.concatenate([left, jnp.zeros((64, 128), F32)], axis=0).T
    owner_of = lax.div(labels[...], 2)
    chosen = (iota((128, held), 0) == owner_of).astype(F32).astype(BF16)
    spread_out = jnp.zeros((128, held), F32)
    for _ in range(3):
        term = left.astype(BF16)
        spread_out = spread_out + jnp.dot(term, chosen, preferred_element_type=F32)
        left = left - term.astype(F32)
    hit = lax.rem(iota((128, held), 0), CAP) == position
    out[...] = jnp.sum(jnp.where(hit, spread_out, 0.0), axis=0, keepdims=True)

    @pl.when(is_owner)
    def _():
        arrived(src.at[pl.ds(0, 63 * CAP)], send_sem)
        arrived(marks.at[pl.ds(0, 63)], mark_send_sem)
        arrived(rows.at[pl.ds(0, 4)], pair_send_sem)
        arrived(row_marks_in.at[pl.ds(0, 4)], pair_mark_send_sem)

        arrived(row_marks.at[0, pl.ds(0, 15 * 16)], result_send_sem)

    @pl.when(jnp.logical_not(is_owner))
    def _():
        arrived(src, send_sem)
        arrived(marks, mark_send_sem)

    arrived(back.at[pl.ds(1, 7)], back_send_sem)


def shards(embeddings, labels):
    held = embeddings.shape[0]
    dma = pltpu.SemaphoreType.DMA
    best = pl.pallas_call(
        kernel,
        out_shape=jax.ShapeDtypeStruct((1, held), F32),
        in_specs=[pl.BlockSpec(memory_space=pl.ANY), pl.BlockSpec(memory_space=pltpu.VMEM)],
        out_specs=pl.BlockSpec(memory_space=pltpu.VMEM),
        scratch_shapes=[
            pltpu.VMEM((held, D), BF16),
            pltpu.VMEM((STEPS * 8 * CAP, D), BF16),
            pltpu.VMEM((64, 128), F32),
            pltpu.VMEM((STEPS, 2 * GROUP, D), BF16),
            pltpu.VMEM((STEPS, 32, 128), F32),
            pltpu.VMEM((STEPS, 2 * GROUP, 128), F32),
            pltpu.VMEM((STEPS, 8, GROUP), F32),
            pltpu.VMEM((STEPS, 8, GROUP), F32),
            pltpu.VMEM((16, 128), F32),
            pltpu.VMEM((8, 16, 128), F32),
            pltpu.VMEM((NZ, 8, 128), F32),
            pltpu.VMEM((NZ, 8, 128), F32),
            dma, dma, dma((STEPS,)), dma, dma((STEPS,)), dma, dma((STEPS,)), dma, dma((STEPS,)), dma, dma, dma, dma,
        ],
        compiler_params=pltpu.CompilerParams(
            collective_id=0, has_side_effects=True, vmem_limit_bytes=48 * 2**20
        ),
    )(embeddings, labels.reshape(1, held))
    return best.reshape(held)


def solution(mesh):
    in_specs = (P(("grp", "blk"), None), P(("grp", "blk")))
    out_specs = P(("grp", "blk"))
    return jax.shard_map(shards, mesh=mesh, in_specs=in_specs, out_specs=out_specs, check_vma=False)
```

time: 210 us -> 90.2 us (0.43)
  Pallas kernels: 0 us -> 87.6 us
  blocking collectives: 75.5 us -> 0 us
  waiting for transfers between devices: 69.6 us -> 0 us
  starting transfers between devices: 15.8 us -> 0 us
  matrix products: 15.5 us -> 0 us
  between operations: 13.5 us -> 0.01 us
  other arithmetic: 10.4 us -> 0 us
  local copies, waits for them, and re-layouts: 8.78 us -> 2.49 us
    pallas_call x0 -> x1, Pallas kernels: none -> 87.6 us  [shards(): pl.pallas_call(kernel, out_shape=jax.ShapeDtypeStruct((1, held), F32), in...]
    all_to_all x1 -> x0, blocking collectives: 63.4 us -> none  [shards(): lax.all_to_all(outgoing.reshape(owners, capacity, -1), 'blk', split_axis=...]
    all_gather x1 -> x0, waiting for transfers between devices: 50.4 us -> none  [shards(): lax.all_gather(mine, 'grp', axis=0, tiled=True)]
    all_to_all x2 -> x0, waiting for transfers between devices: 19.2 us -> none  [the longest x1 9.59 us: shards(): lax.all_to_all(out_marks.reshape(owners, capacity), 'blk', split_axis=0,...]
    all_to_all x2 -> x0, starting transfers between devices: 15.8 us -> none  [the longest x1 10.5 us: shards(): lax.all_to_all(best.reshape(owners, capacity), 'blk', split_axis=0, conca...]
    dot_general x1 -> x0, matrix products: 15.5 us -> none  [masked_tile(): scores = jnp.dot(left, right.T, preferred_element_type=jnp.float32)]
    all_gather x1 -> x0, blocking collectives: 12.2 us -> none  [shards(): lax.all_gather(my_marks, 'grp', axis=0, tiled=True)]
    scatter x1 -> x0, other arithmetic: 3.97 us -> none  [shards(): jnp.zeros((owners * capacity, unit.shape[1]), jnp.bfloat16).at[flat]]
  transfers between devices with their start and end apart: 3 -> 0, of which waited for: 3 -> 0; matrix products, arithmetic and copies ran while one was open for 2% -> 0% of each run, Pallas kernels for 0% -> 0%
where the time goes in v1:
time: 90.2 us; the launch traced here: 90.1 us
  Pallas kernels  87.6 us (97%)
  local copies, waits for them, and re-layouts  2.49 us (3%)
    pallas_call x1, Pallas kernels, shards(): pl.pallas_call(kernel, out_shape=jax.ShapeDtypeStruct((1, held), F32), in...  87.6 us
    unnamed x5, local copies, waits for them, and re-layouts  2.49 us

profile of v1, /device:TPU:2, one launch (start us, length us, event | category | flops | bytes accessed | tf_op | source)
XLA Modules:
  0.0 90.1 jit_solution(15621701893122065225)
XLA Ops:
  0.0 0.0 copy-start
  0.0 1.2 %copy-done = bf16[512,1024]{1,0:T(8,128)(2,1)S(1)} copy-done((bf16[512,1024]{1,0:T(8,128)(2,1)S(1)}, bf16[512,1024]{1,0:T(8,128)(2,1)}, u32[]{:S(2)}) %copy-start) | copy-done | bytes 1048600
  1.2 0.0 copy-start.1
  1.2 0.7 copy-done.1
  1.9 87.6 %shard_map.28 = f32[1,512]{1,0:T(1,128)S(1)} custom-call(bf16[512,1024]{1,0:T(8,128)(2,1)S(1)} %copy-done, s32[1,512]{1,0:T(1,128)S(1)} %bitcast.3), custom_call_target="tpu_custom_call" | custom-call | tf_op jit(solution)/shard_map/pallas_call | solution.py:283
  89.5 0.6 copy.4
Async XLA Ops:
  0.0 1.2 %copy-start = (bf16[512,1024]{1,0:T(8,128)(2,1)S(1)}, bf16[512,1024]{1,0:T(8,128)(2,1)}, u32[]{:S(2)}) copy-start(bf16[512,1024]{1,0:T(8,128)(2,1)} %emb_hbm.1) | copy-start | bytes 3145732
  1.2 0.7 copy-start.1

commit v2 on v1

--- a/solution.py
+++ b/solution.py
@@ -16,6 +16,8 @@
 STEPS = 8
 GROUP = 256
 D = 1024
+UNROLLED = 2
+LOAD = 128
 
 
 def place():
@@ -46,8 +48,8 @@
 
 
 def kernel(
-    emb_hbm, labels, out, emb, src, marks, rows, row_marks_in, row_marks, col_marks, best, result, results, back, backs,
-    load_sem, send_sem, recv_sem, mark_send_sem, mark_recv_sem, pair_send_sem, pair_recv_sem, pair_mark_send_sem,
+    emb_hbm, labels_hbm, out, emb, labels, src, marks, rows, row_marks_in, row_marks, col_marks, best, result, results, back, backs,
+    load_sem, label_sem, send_sem, recv_sem, mark_send_sem, mark_recv_sem, pair_send_sem, pair_recv_sem, pair_mark_send_sem,
     pair_mark_recv_sem, result_send_sem, result_recv_sem, back_send_sem, back_recv_sem,
 ):
     x, y, z, c = place()
@@ -55,27 +57,37 @@
     is_owner = parity == 0
     pair = device(x, y, z, 1 - c)
 
-    load = pltpu.make_async_copy(emb_hbm, emb, load_sem)
-    load.start()
+    label_load = pltpu.make_async_copy(labels_hbm, labels, label_sem)
+    label_load.start()
+
+    def load(n):
+        part = pl.ds(n * LOAD, LOAD)
+        return pltpu.make_async_copy(emb_hbm.at[part], emb.at[part], load_sem.at[n])
+
+    for n in range(emb.shape[0] // LOAD):
+        load(n).start()
     barrier = pltpu.get_barrier_semaphore()
 
     @pl.when(is_owner)
     def _():
+        plane = [device(lax.rem(x + n % NX, NX), lax.rem(y + n // NX, NY), 0, c) for n in range(NX * NY)]
+
         def greet(n, carry):
-            to = device(
-                lax.rem(x + lax.rem(n, NX), NX), lax.rem(y + lax.rem(lax.div(n, NX), NY), NY),
-                lax.rem(z + lax.div(n, NX * NY), NZ), c,
-            )
-            pl.semaphore_signal(barrier, inc=1, device_id=to, device_id_type=MESH)
+            ahead = lax.rem(z + n, NZ) * (2 * NY)
+            for gx, gb in plane:
+                pl.semaphore_signal(barrier, inc=1, device_id=(gx, gb + ahead), device_id_type=MESH)
             return carry
 
-        lax.fori_loop(1, NX * NY * NZ, greet, 0)
+        lax.fori_loop(1, NZ, greet, 0)
+        for gx, gb in plane[1:]:
+            pl.semaphore_signal(barrier, inc=1, device_id=(gx, gb + z * (2 * NY)), device_id_type=MESH)
         pl.semaphore_signal(barrier, inc=1, device_id=pair, device_id_type=MESH)
 
     held = emb.shape[0]
+    before = (iota((held, held), 0) < iota((held, held), 1)).astype(F32).astype(BF16)
+    label_load.wait()
     owner_of = lax.div(labels[...], 2)
     chosen = (iota((64, held), 0) == owner_of).astype(F32)
-    before = (iota((held, held), 0) < iota((held, held), 1)).astype(F32).astype(BF16)
     count = jnp.dot(chosen.astype(BF16), before, preferred_element_type=F32)
     position = jnp.sum(chosen * count, axis=0, keepdims=True).astype(jnp.int32)
     flat = owner_of * CAP + position
@@ -84,16 +96,12 @@
         chosen.astype(BF16), at_lane.astype(BF16), (((1,), (1,)), ((), ())), preferred_element_type=F32
     )
 
-    load.wait()
-
-    def normalise(n, carry):
-        part = pl.ds(n * 64, 64)
+    for n in range(held // LOAD):
+        load(n).wait()
+        part = pl.ds(n * LOAD, LOAD)
         values = emb[part, :].astype(F32)
         scale = lax.rsqrt(jnp.sum(values * values, axis=1, keepdims=True) + 1e-06)
         emb[part, :] = (values * scale).astype(BF16)
-        return carry
-
-    lax.fori_loop(0, held // 64, normalise, 0)
 
     def targets(i):
         out = []
@@ -157,7 +165,6 @@
 
     @pl.when(is_owner)
     def _():
-        best[...] = jnp.full(best.shape, -1.0, F32)
         lane = iota((16, 128), 1)
         mine = lax.div(lane, CAP) == lax.rem(iota((16, 128), 0), 8)
         diagonal = lax.rem(iota((16, CAP, 128), 2), 128) == iota((16, CAP, 128), 1)
@@ -176,8 +183,14 @@
             keep = jnp.concatenate([m, m], axis=1) == col_marks[col, 0:1, :]
             if diag:
                 keep = keep & (iota((size, GROUP), 0) != iota((size, GROUP), 1))
-            sim = jnp.where(keep, sim, -1.0)
-            best[col] = jnp.maximum(best[col], jnp.max(sim.reshape(size // 8, 8, GROUP), axis=0))
+            return jnp.max(jnp.where(keep, sim, -1.0).reshape(size // 8, 8, GROUP), axis=0)
+
+        def loop(n, body, init):
+            if isinstance(n, int):
+                for k in range(n):
+                    init = body(k, init)
+                return init
+            return lax.fori_loop(0, n, body, init)
 
         def group(i, carry):
             arrived(rows.at[i, pl.ds(0, GROUP)], recv_sem.at[i])
@@ -192,26 +205,27 @@
             m = spread(i, 0)
             lanes = jnp.sum(jnp.where(mine, m, 0.0).reshape(2, 8, 128), axis=1)
             col_marks[i] = jnp.broadcast_to(jnp.concatenate([lanes[0:1], lanes[1:2]], axis=1), (8, GROUP))
-            tile(i, 0, GROUP, i, diag=True)
-
-            def earlier(k, carry):
-                tile(k, 0, 2 * GROUP, i)
-                tile(i, 0, GROUP, k)
-                return carry
-
-            lax.fori_loop(0, i, earlier, 0)
+
+            def earlier(k, top):
+                best[k] = jnp.maximum(best[k], tile(i, 0, GROUP, k))
+                return jnp.maximum(top, tile(k, 0, 2 * GROUP, i))
+
+            top = loop(i, earlier, tile(i, 0, GROUP, i, diag=True))
             arrived(rows.at[i, pl.ds(GROUP, GROUP)], pair_recv_sem.at[i])
             arrived(row_marks_in.at[i, pl.ds(16, 16)], pair_mark_recv_sem.at[i])
             spread(i, 1)
-
-            def all_columns(k, carry):
-                tile(i, GROUP, GROUP, k)
+            best[i] = jnp.maximum(top, tile(i, GROUP, GROUP, i))
+
+            def others(k, carry):
+                best[k] = jnp.maximum(best[k], tile(i, GROUP, GROUP, k))
                 return carry
 
-            lax.fori_loop(0, i + 1, all_columns, 0)
+            loop(i, others, 0)
             return carry
 
-        lax.fori_loop(0, STEPS, group, 0)
+        lax.fori_loop(0, STEPS - UNROLLED, group, 0)
+        for i in range(STEPS - UNROLLED, STEPS):
+            group(i, 0)
         for i in range(STEPS):
             top = jnp.max(best[i], axis=0, keepdims=True)
             result[pl.ds(2 * i, 1), :] = top[:, 0:128]
@@ -283,10 +297,11 @@
     best = pl.pallas_call(
         kernel,
         out_shape=jax.ShapeDtypeStruct((1, held), F32),
-        in_specs=[pl.BlockSpec(memory_space=pl.ANY), pl.BlockSpec(memory_space=pltpu.VMEM)],
+        in_specs=[pl.BlockSpec(memory_space=pl.ANY)] * 2,
         out_specs=pl.BlockSpec(memory_space=pltpu.VMEM),
         scratch_shapes=[
             pltpu.VMEM((held, D), BF16),
+            pltpu.VMEM((1, held), jnp.int32),
             pltpu.VMEM((STEPS * 8 * CAP, D), BF16),
             pltpu.VMEM((64, 128), F32),
             pltpu.VMEM((STEPS, 2 * GROUP, D), BF16),
@@ -298,10 +313,10 @@
             pltpu.VMEM((8, 16, 128), F32),
             pltpu.VMEM((NZ, 8, 128), F32),
             pltpu.VMEM((NZ, 8, 128), F32),
-            dma, dma, dma((STEPS,)), dma, dma((STEPS,)), dma, dma((STEPS,)), dma, dma((STEPS,)), dma, dma, dma, dma,
+            dma((held // LOAD,)), dma, dma, dma((STEPS,)), dma, dma((STEPS,)), dma, dma((STEPS,)), dma, dma((STEPS,)), dma, dma, dma, dma,
         ],
         compiler_params=pltpu.CompilerParams(
-            collective_id=0, has_side_effects=True, vmem_limit_bytes=48 * 2**20
+            collective_id=0, has_side_effects=True, vmem_limit_bytes=62 * 2**20
         ),
     )(embeddings, labels.reshape(1, held))
     return best.reshape(held)

time: 90.2 us -> 82.6 us (0.916)
  Pallas kernels: 87.6 us -> 81.3 us
  local copies, waits for them, and re-layouts: 2.49 us -> 1.26 us
    pallas_call x1, Pallas kernels: 87.6 us -> 81.3 us  [shards(): pl.pallas_call(kernel, out_shape=jax.ShapeDtypeStruct((1, held), F32), in...]
    unnamed x5 -> x1, local copies, waits for them, and re-layouts: 2.49 us -> 1.26 us
where the time goes in v2:
time: 82.6 us; the launch traced here: 82.5 us
  Pallas kernels  81.3 us (98%)
  local copies, waits for them, and re-layouts  1.26 us (2%)
    pallas_call x1, Pallas kernels, shards(): pl.pallas_call(kernel, out_shape=jax.ShapeDtypeStruct((1, held), F32), in...  81.3 us

profile of v2, /device:TPU:2, one launch (start us, length us, event | category | flops | bytes accessed | tf_op | source)
XLA Modules:
  0.0 82.5 jit_solution(10342562953520006016)
XLA Ops:
  0.0 81.3 %shard_map.28 = f32[1,512]{1,0:T(1,128)} custom-call(bf16[512,1024]{1,0:T(8,128)(2,1)} %emb_hbm.1, s32[1,512]{1,0:T(1,128)} %bitcast.3), custom_call_target="tpu_custom_call" | custom-call | tf_op jit(solution)/shard_map/pallas_call | solution.py:297
  81.3 1.3 %copy.4 = f32[512]{0:T(512)} copy(f32[512]{0:T(512)} %bitcast.2) | data formatting | bytes 4096

commit v3 on v2

--- a/solution.py
+++ b/solution.py
@@ -48,9 +48,9 @@
 
 
 def kernel(
-    emb_hbm, labels_hbm, out, emb, labels, src, marks, rows, row_marks_in, row_marks, col_marks, best, result, results, back, backs,
+    emb_hbm, labels_hbm, out, emb, labels, src, marks, rows, row_marks_in, row_marks, col_marks, best, result, results,
     load_sem, label_sem, send_sem, recv_sem, mark_send_sem, mark_recv_sem, pair_send_sem, pair_recv_sem, pair_mark_send_sem,
-    pair_mark_recv_sem, result_send_sem, result_recv_sem, back_send_sem, back_recv_sem,
+    pair_mark_recv_sem, result_send_sem, result_recv_sem,
 ):
     x, y, z, c = place()
     parity = lax.rem(x + y + z, 2)
@@ -230,31 +230,37 @@
             top = jnp.max(best[i], axis=0, keepdims=True)
             result[pl.ds(2 * i, 1), :] = top[:, 0:128]
             result[pl.ds(2 * i + 1, 1), :] = top[:, 128:256]
-        me = y * 2 + lax.div(x, 2)
-        pltpu.make_async_copy(result, results.at[me], result_recv_sem).start()
-        for n in range(1, NX * NY):
-            where = device(lax.rem(x + n % NX, NX), lax.rem(y + n // NX, NY), z, c)
-            remote(result, results.at[me], result_send_sem, result_recv_sem, where).start()
+        me = z * 8 + y * 2 + lax.div(x, 2)
+        line = []
+        for n in range(NX * NY):
+            dx, dy = n % NX, n // NX
+            sx, sy = lax.rem(x - dx + NX, NX), lax.rem(y - dy + NY, NY)
+            line.append((dy * 2 + dx // 2, device(sx, sy, 0, c)))
+
+        def give(sz, carry):
+            dz = lax.rem(z - sz + NZ, NZ)
+            t = jnp.where(dz <= NZ // 2, jnp.maximum(2 * dz - 1, 0), 2 * NZ - 2 * dz)
+            for n, (j, (gx, gb)) in enumerate(line):
+                i = lax.rem(t - j + 8, 8)
+                ours, theirs = result.at[pl.ds(2 * i + j // 4, 1)], results.at[pl.ds(me, 1)]
+
+                def away(ours=ours, theirs=theirs, where=(gx, gb + sz * (2 * NY))):
+                    remote(ours, theirs, result_send_sem, result_recv_sem, where).start()
+
+                if n == 0:
+
+                    @pl.when(sz == z)
+                    def _():
+                        pltpu.make_async_copy(ours, theirs, result_recv_sem).start()
+
+                    pl.when(sz != z)(away)
+                else:
+                    away()
+            return carry
+
+        lax.fori_loop(0, NZ, give, 0)
 
     arrived(results, result_recv_sem)
-    for o in range(8):
-        oy = o // 2
-        ox = 2 * (o % 2) + lax.rem(oy + z, 2)
-        dx = lax.rem(ox - x + NX, NX)
-        j = lax.rem(oy - y + NY, NY) * 2 + lax.div(dx, 2)
-
-        def turn(t, carry):
-            i = lax.rem(t - j + 8, 8)
-            back[t, pl.ds(o, 1), :] = results[o, pl.ds(2 * i + lax.div(j, 4), 1), :]
-            return carry
-
-        lax.fori_loop(0, NZ, turn, 0)
-    pltpu.make_async_copy(back.at[0], backs.at[z], back_recv_sem).start()
-    for t in range(1, NZ):
-        dz = (t + 1) // 2 if t % 2 else (NZ - t // 2) % NZ
-        where = device(x, y, lax.rem(z - dz + NZ, NZ), c)
-        remote(back.at[t], backs.at[z], back_send_sem, back_recv_sem, where).start()
-    arrived(backs, back_recv_sem)
 
     b = iota((64, 128), 0)
     oz, oy = lax.div(b, 8), lax.rem(lax.div(b, 2), NY)
@@ -262,7 +268,7 @@
     dx = lax.rem(ox - x + NX, NX)
     j = lax.rem(oy - y + NY, NY) * 2 + lax.div(dx, 2)
     ours = lax.div(iota((64, 128), 1), CAP) == lax.rem(j, 4) * 2 + lax.rem(dx, 2)
-    left = jnp.where(ours, backs[...].reshape(64, 128), 0.0)
+    left = jnp.where(ours, results[...], 0.0)
     left = jnp.concatenate([left, jnp.zeros((64, 128), F32)], axis=0).T
     owner_of = lax.div(labels[...], 2)
     chosen = (iota((128, held), 0) == owner_of).astype(F32).astype(BF16)
@@ -281,14 +287,12 @@
         arrived(rows.at[pl.ds(0, 4)], pair_send_sem)
         arrived(row_marks_in.at[pl.ds(0, 4)], pair_mark_send_sem)
 
-        arrived(row_marks.at[0, pl.ds(0, 15 * 16)], result_send_sem)
+        arrived(row_marks.at[0, pl.ds(0, 127)], result_send_sem)
 
     @pl.when(jnp.logical_not(is_owner))
     def _():
         arrived(src, send_sem)
         arrived(marks, mark_send_sem)
-
-    arrived(back.at[pl.ds(1, 7)], back_send_sem)
 
 
 def shards(embeddings, labels):
@@ -310,10 +314,8 @@
             pltpu.VMEM((STEPS, 8, GROUP), F32),
             pltpu.VMEM((STEPS, 8, GROUP), F32),
             pltpu.VMEM((16, 128), F32),
-            pltpu.VMEM((8, 16, 128), F32),
-            pltpu.VMEM((NZ, 8, 128), F32),
-            pltpu.VMEM((NZ, 8, 128), F32),
-            dma((held // LOAD,)), dma, dma, dma((STEPS,)), dma, dma((STEPS,)), dma, dma((STEPS,)), dma, dma((STEPS,)), dma, dma, dma, dma,
+            pltpu.VMEM((64, 128), F32),
+            dma((held // LOAD,)), dma, dma, dma((STEPS,)), dma, dma((STEPS,)), dma, dma((STEPS,)), dma, dma((STEPS,)), dma, dma,
         ],
         compiler_params=pltpu.CompilerParams(
             collective_id=0, has_side_effects=True, vmem_limit_bytes=62 * 2**20

time: 82.6 us -> 79.5 us (0.962)
  Pallas kernels: 81.3 us -> 78.2 us
    pallas_call x1, Pallas kernels: 81.3 us -> 78.2 us  [shards(): pl.pallas_call(kernel, out_shape=jax.ShapeDtypeStruct((1, held), F32), in...]
where the time goes in v3:
time: 79.5 us; the launch traced here: 79.4 us
  Pallas kernels  78.2 us (98%)
  local copies, waits for them, and re-layouts  1.26 us (2%)
    pallas_call x1, Pallas kernels, shards(): pl.pallas_call(kernel, out_shape=jax.ShapeDtypeStruct((1, held), F32), in...  78.2 us

profile of v3, /device:TPU:2, one launch (start us, length us, event | category | flops | bytes accessed | tf_op | source)
XLA Modules:
  0.0 79.4 jit_solution(3911114484445087892)
XLA Ops:
  0.0 78.2 %shard_map.28 = f32[1,512]{1,0:T(1,128)} custom-call(bf16[512,1024]{1,0:T(8,128)(2,1)} %emb_hbm.1, s32[1,512]{1,0:T(1,128)} %bitcast.3), custom_call_target="tpu_custom_call" | custom-call | tf_op jit(solution)/shard_map/pallas_call | solution.py:301
  78.2 1.3 %copy.4 = f32[512]{0:T(512)} copy(f32[512]{0:T(512)} %bitcast.2) | data formatting | bytes 4096

commit v4 on v3

--- a/solution.py
+++ b/solution.py
@@ -272,11 +272,12 @@
     left = jnp.concatenate([left, jnp.zeros((64, 128), F32)], axis=0).T
     owner_of = lax.div(labels[...], 2)
     chosen = (iota((128, held), 0) == owner_of).astype(F32).astype(BF16)
-    spread_out = jnp.zeros((128, held), F32)
+    terms = []
     for _ in range(3):
-        term = left.astype(BF16)
-        spread_out = spread_out + jnp.dot(term, chosen, preferred_element_type=F32)
-        left = left - term.astype(F32)
+        terms.append(left.astype(BF16))
+        left = left - terms[-1].astype(F32)
+    found = jnp.dot(jnp.concatenate(terms, axis=0), chosen, preferred_element_type=F32)
+    spread_out = found[0:128] + found[128:256] + found[256:384]
     hit = lax.rem(iota((128, held), 0), CAP) == position
     out[...] = jnp.sum(jnp.where(hit, spread_out, 0.0), axis=0, keepdims=True)
 
@@ -318,7 +319,7 @@
             dma((held // LOAD,)), dma, dma, dma((STEPS,)), dma, dma((STEPS,)), dma, dma((STEPS,)), dma, dma((STEPS,)), dma, dma,
         ],
         compiler_params=pltpu.CompilerParams(
-            collective_id=0, has_side_effects=True, vmem_limit_bytes=62 * 2**20
+            collective_id=0, has_side_effects=True, vmem_limit_bytes=55000 * 1024
         ),
     )(embeddings, labels.reshape(1, held))
     return best.reshape(held)

time: 79.5 us -> 78.9 us (level)
  no operation moved by 1% of the time
where the time goes in v4:
time: 78.9 us; the launch traced here: 78.8 us
  Pallas kernels  77.6 us (98%)
  local copies, waits for them, and re-layouts  1.26 us (2%)
    pallas_call x1, Pallas kernels, shards(): pl.pallas_call(kernel, out_shape=jax.ShapeDtypeStruct((1, held), F32), in...  77.6 us

profile of v4, /device:TPU:2, one launch (start us, length us, event | category | flops | bytes accessed | tf_op | source)
XLA Modules:
  0.0 78.8 jit_solution(9978635379036848368)
XLA Ops:
  0.0 0.0 copy-start
  0.0 0.7 copy-done
  0.7 77.6 %shard_map.28 = f32[1,512]{1,0:T(1,128)S(1)} custom-call(bf16[512,1024]{1,0:T(8,128)(2,1)} %emb_hbm.1, s32[1,512]{1,0:T(1,128)S(1)} %bitcast.3), custom_call_target="tpu_custom_call" | custom-call | tf_op jit(solution)/shard_map/pallas_call | solution.py:302
  78.3 0.6 copy.4
Async XLA Ops:
  0.0 0.7 copy-start

commit v5 on v4

--- a/solution.py
+++ b/solution.py
@@ -78,9 +78,9 @@
                 pl.semaphore_signal(barrier, inc=1, device_id=(gx, gb + ahead), device_id_type=MESH)
             return carry
 
-        lax.fori_loop(1, NZ, greet, 0)
         for gx, gb in plane[1:]:
             pl.semaphore_signal(barrier, inc=1, device_id=(gx, gb + z * (2 * NY)), device_id_type=MESH)
+        lax.fori_loop(1, NZ, greet, 0, unroll=True)
         pl.semaphore_signal(barrier, inc=1, device_id=pair, device_id_type=MESH)
 
     held = emb.shape[0]
@@ -195,9 +195,9 @@
         def group(i, carry):
             arrived(rows.at[i, pl.ds(0, GROUP)], recv_sem.at[i])
             arrived(row_marks_in.at[i, pl.ds(0, 16)], mark_recv_sem.at[i])
-            remote(
-                rows.at[i, pl.ds(0, GROUP)], rows.at[i, pl.ds(GROUP, GROUP)], pair_send_sem, pair_recv_sem.at[i], pair
-            ).start()
+            for n in range(4):
+                part, there = pl.ds(n * 64, 64), pl.ds(GROUP + n * 64, 64)
+                remote(rows.at[i, part], rows.at[i, there], pair_send_sem, pair_recv_sem.at[i], pair).start()
             remote(
                 row_marks_in.at[i, pl.ds(0, 16)], row_marks_in.at[i, pl.ds(16, 16)], pair_mark_send_sem,
                 pair_mark_recv_sem.at[i], pair,

time: 78.9 us -> 78.7 us (level)
  no operation moved by 1% of the time
where the time goes in v5:
time: 78.7 us; the launch traced here: 78.5 us
  Pallas kernels  77.3 us (98%)
  local copies, waits for them, and re-layouts  1.26 us (2%)
    pallas_call x1, Pallas kernels, shards(): pl.pallas_call(kernel, out_shape=jax.ShapeDtypeStruct((1, held), F32), in...  77.3 us

profile of v5, /device:TPU:2, one launch (start us, length us, event | category | flops | bytes accessed | tf_op | source)
XLA Modules:
  0.0 78.5 jit_solution(4280747958786626971)
XLA Ops:
  0.0 0.0 copy-start
  0.0 0.7 copy-done
  0.7 77.3 %shard_map.28 = f32[1,512]{1,0:T(1,128)S(1)} custom-call(bf16[512,1024]{1,0:T(8,128)(2,1)} %emb_hbm.1, s32[1,512]{1,0:T(1,128)S(1)} %bitcast.3), custom_call_target="tpu_custom_call" | custom-call | tf_op jit(solution)/shard_map/pallas_call | solution.py:302
  78.0 0.6 copy.4
Async XLA Ops:
  0.0 0.7 copy-start
